TPU v7x, 32 devices: a whole 2x2x4 slice. The times are simulated.
32 devices in a mesh: mode: 8 (over y, x, core), elem: 4 (over z).
Axes of the slice: x: 2, y: 2, z: 4, core: 2. Of those that a mesh axis runs over, the one named last changes fastest.
Arguments:
- velocity: float32 [3, 128, 4096], P(None, 'mode', 'elem'), may hold values from -1.5 to 1.5
- metric_main: float32 [2, 4096], P(None, 'elem'), may hold values from 0.5 to 1.5
- metric_cross: float32 [2, 4096], P(None, 'elem'), may hold values from -0.5 to 0.5
- stiffness: float32 [4096, 512], P('elem'), as said below
- mass: float32 [4096], P('elem'), may hold values from 0.5 to 2
- precond: float32 [64, 4096, 512], P('mode', 'elem'), as said below
- trace_map: int32 [8, 2, 32], P('elem'), may hold values from 0 to 511, as said below
Outputs:
- new_velocity: float32 [3, 128, 4096], P(None, 'mode', 'elem')
Inputs may be any that keep to these rules, and one draw needn't show every extreme that they name: trace_map[q, 0] and trace_map[q, 1] together hold 64 distinct points of patch q; slot j of trace_map[q, 1] and slot j of trace_map[q + 1, 0] are the same plane point. `stiffness`: each 512 x 512 block is symmetric. `precond`: one 512 x 512 matrix for each mode and patch.
All inputs are finite; a program needn't handle non-finite values.
Results may differ from a plain program's by a relative error of at most 0.0003.
Values sent between devices are 32-bit elements; how exact they have to be, the bound alone decides.
A program may use at most 128 MiB of HBM per device.

v0:
```python
import functools
import math

import jax
import jax.numpy as jnp
import numpy as np
from jax import lax
from jax.experimental import pallas as pl
from jax.experimental.pallas import tpu as pltpu
from jax.sharding import PartitionSpec as P

NZ = 256
STEPS = 4
ITERS = 4
LANES = 128

viscous_step = 0.5
time_step = 0.02
relaxation = 0.8
f32 = jnp.float32
bf16 = jnp.bfloat16
MODES = 64
KZ = 128
highest_precision = lax.Precision.HIGHEST


def chebyshev_matrix():
    node_points = np.cos(np.pi * np.arange(8) / 7.0)
    weights = np.where((np.arange(8) == 0) | (np.arange(8) == 7), 2.0, 1.0)
    parity = np.where((np.arange(8)[:, None] + np.arange(8)[None, :]) % 2 == 0, 1.0, -1.0)
    identity = np.eye(8)
    spacing = node_points[:, None] - node_points[None, :] + identity
    off_diagonal = weights[:, None] / weights[None, :] * parity / spacing * (1.0 - identity)
    return off_diagonal - identity * off_diagonal.sum(axis=1)[:, None]


def pair(table):
    table = np.asarray(table, np.float32)
    high = table.astype(bf16)
    low = (table - high.astype(np.float32)).astype(bf16)
    return high, low


def spanwise_tables(modes):
    angle = 2.0 * math.pi / NZ * (np.arange(NZ)[:, None] * np.arange(modes)[None, :] % NZ)
    rate = 4.0 * np.arange(modes) / modes
    cosine, sine = np.cos(angle), np.sin(angle)
    basis = np.concatenate([cosine, sine], axis=1)
    slope = np.concatenate([-rate * sine, rate * cosine], axis=1)
    factor = np.full(2 * modes, 2.0 / NZ)
    factor[0] = 1.0 / NZ
    forward = basis.T * factor[:, None]

    def left_three(table):
        high, low = pair(table)
        return np.concatenate([high, low, high], axis=1)

    return left_three(basis), left_three(slope), np.stack(pair(forward))


def plane_tables():
    chebyshev = chebyshev_matrix()
    position = np.arange(LANES)
    column, row, element = position % 8, position // 8 % 8, position // 64
    same = element[:, None] == element[None, :]
    xi = np.where(same & (row[:, None] == row[None, :]), chebyshev.T[column][:, column], 0.0)
    eta = np.where(same & (column[:, None] == column[None, :]), chebyshev.T[row][:, row], 0.0)
    return np.stack(pair(np.concatenate([xi, eta], axis=1)))


def row_order(modes):
    move = np.zeros((modes * 8, 6 * modes), np.float32)
    for field in range(6):
        for mode in range(modes):
            move[mode * 8 + field, field * modes + mode] = 1.0
    shuffle = np.zeros((6 * modes, 6 * modes), np.float32)
    for c in range(3):
        for half in range(2):
            for mode in range(modes):
                shuffle[(2 * c + half) * modes + mode, (c * modes + mode) * 2 + half] = 1.0
    return [table.astype(bf16) for table in (move, move.T, shuffle, shuffle.T @ move.T)]


def dot(a, b):
    return lax.dot_general(a, b, (((1,), (0,)), ((), ())), preferred_element_type=f32)


def split(value):
    high = value.astype(bf16)
    return high, (value - high.astype(f32)).astype(bf16)


def both(value):
    high = value.astype(bf16).astype(f32)
    low = value - high
    tiles = []
    for start in range(0, value.shape[0], 8):
        tiles += [high[start : start + 8], low[start : start + 8]]
    return jnp.concatenate(tiles, axis=0).astype(bf16)


def folded(value):
    tiles = [
        value[start : start + 8] + value[start + 8 : start + 16]
        for start in range(0, value.shape[0], 16)
    ]
    return jnp.concatenate(tiles, axis=0)


def product(value, high, low):
    parts = both(value)
    return folded(dot(parts, high) + dot(parts, low))


def moved(value, one_hot):
    return folded(dot(both(value), one_hot))


def reordered(move, value):
    high, low = split(value)
    return dot(move, high) + dot(move, low)


def exactly(move, value):
    high, low = split(value)
    rest = (value - high.astype(f32) - low.astype(f32)).astype(bf16)
    return dot(move, high) + (dot(move, low) + dot(move, rest))


def kernel(
    ranks,
    depth,
    modes,
    patches,
    width,
    trace,
    share,
    velocity,
    metric_main,
    metric_cross,
    stiffness,
    mass,
    slots,
    tables,
    forward,
    plane,
    move,
    back,
    enter,
    leave,
    precond,
    out,
    raw,
    inverse_high,
    inverse_low,
    stiff_high,
    stiff_low,
    across,
    edge_high,
    edge_low,
    rows_high,
    rows_low,
    gate_high,
    gate_low,
    pick,
    pick_back,
    corner_out,
    corner_in,
    corner_high,
    corner_low,
    state,
    coef,
    hat,
    returned,
    local,
    damped,
    weight,
    iterate,
    note_out,
    note_in,
    raw_sem,
    own_sem,
    coef_send,
    hat_send,
    coef_sem,
    hat_sem,
    note_send,
    note_recv,
    corner_send,
    corner_recv,
):
    me = lax.axis_index("mode")
    place = lax.axis_index("elem")
    has = (place > 0, place < depth - 1)
    beside = (place - 1, place + 1)
    rows = 8 * modes
    wide = modes * trace

    def patch_of(p):
        return pl.ds(p * width, width)

    for k in range(modes):
        for p in range(patches):
            pltpu.make_async_copy(
                precond.at[k, patch_of(p), :], raw.at[k, patch_of(p), :], raw_sem.at[k, p]
            ).start()

    note_in[...] = jnp.zeros_like(note_in)
    corner_in[...] = jnp.zeros_like(corner_in)
    state[...] = exactly(enter[...], velocity[...].reshape(6 * modes, patches * width)).reshape(
        6, modes, patches * width
    )

    barrier = pltpu.get_barrier_semaphore()
    for offset in range(1, ranks):
        pl.semaphore_signal(
            barrier, 1, device_id={"mode": lax.rem(me + offset, ranks)},
            device_id_type=pl.DeviceIdType.MESH,
        )
    for side in range(2):
        @pl.when(has[side])
        def _():
            pl.semaphore_signal(
                barrier, 1, device_id={"elem": beside[side]}, device_id_type=pl.DeviceIdType.MESH
            )
    near_side = (jnp.minimum(place, 1), jnp.minimum(depth - 1 - place, 1))
    near_count = [side.astype(f32) for side in near_side]
    pl.semaphore_wait(barrier, ranks - 1 + near_side[0] + near_side[1])

    def points_of(rank):
        return pl.ds(pl.multiple_of(rank * share, share), share)

    def modes_of(rank):
        return pl.ds(pl.multiple_of(rank * modes, modes), modes)

    def coef_copy(offset):
        to = lax.rem(me + offset, ranks)
        return pltpu.make_async_remote_copy(
            src_ref=state.at[:, :, points_of(to)],
            dst_ref=coef.at[:, modes_of(me), :],
            send_sem=coef_send.at[offset],
            recv_sem=coef_sem.at[offset],
            device_id={"mode": to},
            device_id_type=pl.DeviceIdType.MESH,
        )

    def hat_copy(offset, c):
        to = lax.rem(me + offset, ranks)
        return pltpu.make_async_remote_copy(
            src_ref=hat.at[pl.ds(2 * c, 2), modes_of(to), :],
            dst_ref=returned.at[pl.ds(2 * c, 2), :, points_of(me)],
            send_sem=hat_send.at[c, offset],
            recv_sem=hat_sem.at[c, offset],
            device_id={"mode": to},
            device_id_type=pl.DeviceIdType.MESH,
        )

    def own_coef():
        return pltpu.make_async_copy(
            state.at[:, :, points_of(me)], coef.at[:, modes_of(me), :], own_sem.at[0]
        )

    def own_hat():
        return pltpu.make_async_copy(
            hat.at[:, modes_of(me), :], returned.at[:, :, points_of(me)], own_sem.at[1]
        )

    def send_coef():
        for offset in range(1, ranks):
            coef_copy(offset).start()
        own_coef().start()

    def note_copy(side, slot):
        return pltpu.make_async_remote_copy(
            src_ref=note_out.at[side],
            dst_ref=note_in.at[slot, 1 - side],
            send_sem=note_send.at[side],
            recv_sem=note_recv.at[slot, 1 - side],
            device_id={"elem": beside[side]},
            device_id_type=pl.DeviceIdType.MESH,
        )

    def corner_copy(side):
        return pltpu.make_async_remote_copy(
            src_ref=corner_out.at[side],
            dst_ref=corner_in.at[1 - side],
            send_sem=corner_send.at[side],
            recv_sem=corner_recv.at[1 - side],
            device_id={"elem": beside[side]},
            device_id_type=pl.DeviceIdType.MESH,
        )

    def note_wait(side, slot):
        note_copy(side, slot).wait_send()
        pltpu.make_async_remote_copy(
            src_ref=note_out.at[side],
            dst_ref=note_in.at[slot, side],
            send_sem=note_send.at[side],
            recv_sem=note_recv.at[slot, side],
            device_id={"elem": beside[side]},
            device_id_type=pl.DeviceIdType.MESH,
        ).wait_recv()

    def corner_wait(side):
        corner_copy(side).wait_send()
        pltpu.make_async_remote_copy(
            src_ref=corner_out.at[side],
            dst_ref=corner_in.at[side],
            send_sem=corner_send.at[side],
            recv_sem=corner_recv.at[side],
            device_id={"elem": beside[side]},
            device_id_type=pl.DeviceIdType.MESH,
        ).wait_recv()

    send_coef()

    edge_patch = (0, patches - 1)
    point = lax.broadcasted_iota(jnp.int32, (width, LANES), 0)
    for p in range(patches):
        stiff_high[p], stiff_low[p] = split(viscous_step * stiffness[patch_of(p), :])
        multiplicity = jnp.ones((1, width), f32)
        for side in range(2):
            for kind in range(2):
                line = (p * 2 + side) * 2 + kind
                one_hot = jnp.where(slots[line : line + 1, :] == point, 1.0, 0.0)
                turned = one_hot.T
                pick[p, side, kind] = one_hot.astype(bf16)
                pick_back[p, side, kind] = turned.astype(bf16)
                if kind == 0:
                    gain = near_count[side] if p == edge_patch[side] else 1.0
                    multiplicity += gain * jnp.sum(turned, axis=0, keepdims=True)
        weight[:, patch_of(p)] = relaxation / (multiplicity * multiplicity)
    for p in range(patches - 1):
        across[p, 0] = dot(pick[p, 1, 0], pick_back[p + 1, 0, 0]).astype(bf16)
        across[p, 1] = dot(pick[p + 1, 0, 0], pick_back[p, 1, 0]).astype(bf16)
    number = lax.broadcasted_iota(jnp.int32, (rows, 1), 0) // 8 + me * modes
    rate = 4.0 * number.astype(f32) / (modes * ranks)
    damped[...] = (1.0 + viscous_step * rate * rate) * mass[...]

    def prepare(k, carry):
        span = pl.ds(pl.multiple_of(k * trace, trace), trace)
        for p in range(patches):
            pltpu.make_async_copy(
                precond.at[k, patch_of(p), :], raw.at[k, patch_of(p), :], raw_sem.at[k, p]
            ).wait()
            block = raw[k, patch_of(p), :]
            high, low = split(block.T)
            inverse_high[k, p] = high
            inverse_low[k, p] = low
            plain_high, plain_low = split(block)
            for side in range(2):
                if p == edge_patch[side]:
                    choose = pick_back[p, side, 0, :trace, :]
                    edge_high[side, span, :] = dot(choose, high).astype(bf16)
                    edge_low[side, span, :] = dot(choose, low).astype(bf16)
                    rows_high[side, span, :] = dot(choose, plain_high)
                    rows_low[side, span, :] = dot(choose, plain_low)
        return carry

    lax.fori_loop(0, modes, prepare, 0)
    for side in range(2):
        choose = pick[edge_patch[side], side, 1]
        corner_out[side] = dot(edge_high[side], choose) + dot(edge_low[side], choose)

        @pl.when(has[side])
        def _():
            corner_copy(side).start()
    for side in range(2):
        gate_high[side, :, :wide] = rows_high[side].T.astype(bf16)
        gate_high[side, :, wide:] = pick[edge_patch[side], side, 0]
        gate_low[side] = rows_low[side].T.astype(bf16)
    for side in range(2):
        @pl.when(has[side])
        def _():
            corner_wait(side)
        corner_high[side], corner_low[side] = split(corner_in[side])

    lane = lax.broadcasted_iota(jnp.int32, (rows, LANES), 1)
    block_mask = (
        lax.broadcasted_iota(jnp.int32, (rows, wide), 0) // 8
        == lax.broadcasted_iota(jnp.int32, (rows, wide), 1) // trace
    )

    def repeated(value):
        total = value
        for turn in range(1, LANES // trace):
            total = total + pltpu.roll(value, turn * trace, 1)
        return total

    def spread(note):
        total = repeated(jnp.where(lane < trace, note, 0.0))
        tiled = jnp.concatenate([total] * (wide // LANES), axis=1)
        return jnp.where(block_mask, tiled, 0.0)

    def noted(parts, side):
        sent = folded(dot(parts, gate_high[side]))
        traced = sent[:, :wide] + folded(dot(parts, gate_low[side]))
        traced = jnp.where(block_mask, traced, 0.0)
        total = traced[:, :LANES]
        for start in range(LANES, wide, LANES):
            total = total + traced[:, start : start + LANES]
        return sent[:, wide:] + jnp.where(lane >= trace, repeated(total), 0.0)

    def advect():
        for offset in range(1, ranks):
            coef_copy(offset).wait_recv()
        own_coef().wait()
        each = 2 * modes * ranks
        fields = coef[...].reshape(3 * each, share)
        high, low = split(fields)
        slopes = dot(high, plane[0]) + dot(low, plane[0]) + dot(high, plane[1])
        xi, eta = slopes[:, :share], slopes[:, share:]
        mine = points_of(me)
        grad_x = metric_main[0:1, mine] * xi + metric_cross[0:1, mine] * eta
        grad_y = metric_cross[1:2, mine] * xi + metric_main[1:2, mine] * eta

        def physical(table, values):
            high, low = split(jnp.concatenate(values, axis=1))
            return dot(table, jnp.concatenate([high, high, low], axis=0))

        def part(value, c):
            return value[c * each : (c + 1) * each]

        plain = physical(tables[...], [part(fields, c) for c in range(3)])
        u, v, w = (plain[:NZ, c * share : (c + 1) * share] for c in range(3))
        for c in range(3):
            slope = physical(tables[:NZ], [part(grad_x, c), part(grad_y, c)])
            advection = (
                u * slope[:, :share]
                + v * slope[:, share:]
                + w * plain[NZ:, c * share : (c + 1) * share]
            )
            high, low = split(advection)
            total = dot(forward[0], high) + dot(forward[0], low) + dot(forward[1], high)
            hat[pl.ds(2 * c, 2)] = total.reshape(2, modes * ranks, share)
            for offset in range(1, ranks):
                hat_copy(offset, c).start()
        own_hat().start()
        for offset in range(1, ranks):
            coef_copy(offset).wait_send()
            for c in range(3):
                hat_copy(offset, c).wait_recv()
        own_hat().wait()
        for offset in range(1, ranks):
            for c in range(3):
                hat_copy(offset, c).wait_send()
        source = (state[...] - time_step * returned[...]).reshape(6 * modes, patches * width)
        local[...] = mass[...] * reordered(move[...], source)

    def assembled(parts):
        result = list(parts)
        for p in range(patches - 1):
            result[p + 1] = result[p + 1] + moved(parts[p], across[p, 0])
            result[p] = result[p] + moved(parts[p + 1], across[p, 1])
        return result

    def sweep(number, first):
        slot = lax.rem(number, 2)
        terms = []
        for p in range(patches):
            term = local[:, patch_of(p)]
            if not first:
                value = iterate[:, patch_of(p)]
                term = (
                    term
                    - product(value, stiff_high[p], stiff_low[p])
                    - damped[:, patch_of(p)] * value
                )
            terms.append(term)
        lines = [both(term) for term in assembled(terms)]
        notes = []
        for side in range(2):
            note = noted(lines[edge_patch[side]], side)
            note_out[side] = note
            notes.append(note)
        for side in range(2):
            @pl.when(has[side])
            def _():
                note_copy(side, slot).start()
        parts = []
        for p in range(patches):
            found = []
            for k in range(modes):
                line = lines[p][k * 16 : (k + 1) * 16]
                found.append(dot(line, inverse_high[k, p]) + dot(line, inverse_low[k, p]))
            parts.append(folded(jnp.concatenate(found, axis=0)))
        near = [product(spread(notes[side]), corner_high[side], corner_low[side]) for side in range(2)]
        for side in range(2):
            @pl.when(has[side])
            def _():
                note_wait(side, slot)
        gains = []
        for side in range(2):
            p = edge_patch[side]
            note = note_in[slot, side]
            parts[p] = parts[p] + product(spread(note), edge_high[side], edge_low[side])
            gains.append(moved(note + near[side], pick_back[p, side, 1]))
        total = assembled(parts)
        for side in range(2):
            p = edge_patch[side]
            total[p] = total[p] + gains[side]
        for p in range(patches):
            step = weight[:, patch_of(p)] * total[p]
            iterate[:, patch_of(p)] = step if first else iterate[:, patch_of(p)] + step

    def later_sweep(number, carry):
        sweep(number, False)
        return carry

    def level(number, carry):
        advect()
        sweep(0, True)
        lax.fori_loop(1, ITERS, later_sweep, 0)
        state[...] = reordered(back[...], iterate[...]).reshape(6, modes, patches * width)

        @pl.when(number < STEPS - 1)
        def _():
            send_coef()

        return carry

    lax.fori_loop(0, STEPS, level, 0)
    out[...] = exactly(leave[...], iterate[...]).reshape(3, 2 * modes, patches * width)


def on_device(velocity, metric_main, metric_cross, stiffness, mass, precond, trace_map):
    ranks, depth = lax.axis_size("mode"), lax.axis_size("elem")
    rows, points = velocity.shape[1:]
    modes = rows // 2
    patches, _, trace = trace_map.shape
    width = stiffness.shape[1]
    share = points // ranks
    if modes % 8 or share != LANES or LANES % trace or (modes * trace) % LANES or patches < 2:
        return general_device(
            velocity, metric_main, metric_cross, stiffness, mass, precond, trace_map
        )
    slots = jnp.stack(
        [
            jnp.pad(trace_map, ((0, 0), (0, 0), (0, LANES - trace)), constant_values=-1),
            jnp.pad(trace_map, ((0, 0), (0, 0), (trace, LANES - 2 * trace)), constant_values=-1),
        ],
        axis=2,
    )
    basis, slope, forward = spanwise_tables(modes * ranks)
    vmem = pl.BlockSpec(memory_space=pltpu.VMEM)
    wide = modes * trace
    blocks = (modes, patches, width, width)
    return pl.pallas_call(
        functools.partial(kernel, ranks, depth, modes, patches, width, trace, share),
        out_shape=jax.ShapeDtypeStruct(velocity.shape, f32),
        in_specs=[vmem] * 13 + [pl.BlockSpec(memory_space=pl.ANY)],
        out_specs=vmem,
        scratch_shapes=[
            pltpu.VMEM((modes, patches * width, width), f32),
            pltpu.VMEM(blocks, bf16),
            pltpu.VMEM(blocks, bf16),
            pltpu.VMEM((patches, width, width), bf16),
            pltpu.VMEM((patches, width, width), bf16),
            pltpu.VMEM((patches - 1, 2, width, width), bf16),
            pltpu.VMEM((2, wide, width), bf16),
            pltpu.VMEM((2, wide, width), bf16),
            pltpu.VMEM((2, wide, width), f32),
            pltpu.VMEM((2, wide, width), f32),
            pltpu.VMEM((2, width, wide + LANES), bf16),
            pltpu.VMEM((2, width, wide), bf16),
            pltpu.VMEM((patches, 2, 2, width, LANES), bf16),
            pltpu.VMEM((patches, 2, 2, LANES, width), bf16),
            pltpu.VMEM((2, wide, LANES), f32),
            pltpu.VMEM((2, wide, LANES), f32),
            pltpu.VMEM((2, wide, LANES), bf16),
            pltpu.VMEM((2, wide, LANES), bf16),
            pltpu.VMEM((6, modes, points), f32),
            pltpu.VMEM((6, modes * ranks, share), f32),
            pltpu.VMEM((6, modes * ranks, share), f32),
            pltpu.VMEM((6, modes, points), f32),
            pltpu.VMEM((8 * modes, points), f32),
            pltpu.VMEM((8 * modes, points), f32),
            pltpu.VMEM((1, points), f32),
            pltpu.VMEM((8 * modes, points), f32),
            pltpu.VMEM((2, 8 * modes, LANES), f32),
            pltpu.VMEM((2, 2, 8 * modes, LANES), f32),
            pltpu.SemaphoreType.DMA((modes, patches)),
            pltpu.SemaphoreType.DMA((2,)),
            pltpu.SemaphoreType.DMA((ranks,)),
            pltpu.SemaphoreType.DMA((3, ranks)),
            pltpu.SemaphoreType.DMA((ranks,)),
            pltpu.SemaphoreType.DMA((3, ranks)),
            pltpu.SemaphoreType.DMA((2,)),
            pltpu.SemaphoreType.DMA((2, 2)),
            pltpu.SemaphoreType.DMA((2,)),
            pltpu.SemaphoreType.DMA((2,)),
        ],
        compiler_params=pltpu.CompilerParams(
            collective_id=0, has_side_effects=True, vmem_limit_bytes=56 * 1024 * 1024
        ),
    )(
        velocity,
        metric_main,
        metric_cross,
        stiffness,
        mass.reshape(1, points),
        slots.reshape(patches * 4, LANES),
        jnp.asarray(np.concatenate([basis, slope], axis=0)),
        jnp.asarray(forward),
        jnp.asarray(plane_tables()),
        *[jnp.asarray(table) for table in row_order(modes)],
        precond,
    )


def shifted(value, axis, steps):
    count = lax.axis_size(axis)
    initial, last = (max(0, -steps), min(count, count - steps))
    return lax.ppermute(value, axis, [(source, source + steps) for source in range(initial, last)])


def general_spanwise():
    spanwise = jnp.arange(NZ, dtype=jnp.int32)
    row_numbers = jnp.arange(KZ, dtype=jnp.int32)
    wavenumber = row_numbers // 2
    product = spanwise[:, None] * wavenumber[None, :] % NZ
    phase_angle = 2.0 * math.pi / NZ * product.astype(jnp.float32)
    is_sine = (row_numbers % 2 == 1)[None, :]
    basis_table = jnp.where(is_sine, jnp.sin(phase_angle), jnp.cos(phase_angle))
    wave_rate = 4.0 * wavenumber.astype(jnp.float32) / MODES
    slope_table = jnp.where(
        is_sine,
        wave_rate[None, :] * jnp.cos(phase_angle),
        -wave_rate[None, :] * jnp.sin(phase_angle),
    )
    norm_factor = jnp.where(row_numbers == 0, 1.0 / NZ, 2.0 / NZ).astype(jnp.float32)
    forward = basis_table.T * norm_factor[:, None]
    return (basis_table, slope_table, forward, wave_rate)


def general_plane(chebyshev):
    position = jnp.arange(128, dtype=jnp.int32)
    node_column = position % 8
    node_row = position // 8 % 8
    element = position // 64
    eight = jnp.arange(8, dtype=jnp.int32)[None, :]
    pick_column = (node_column[:, None] == eight).astype(jnp.float32)
    pick_row = (node_row[:, None] == eight).astype(jnp.float32)
    same_element = element[:, None] == element[None, :]
    along_xi = jnp.dot(
        jnp.dot(pick_column, chebyshev.T, precision=highest_precision),
        pick_column.T,
        precision=highest_precision,
    )
    along_eta = jnp.dot(
        jnp.dot(pick_row, chebyshev.T, precision=highest_precision),
        pick_row.T,
        precision=highest_precision,
    )
    xi_table = jnp.where(same_element & (node_row[:, None] == node_row[None, :]), along_xi, 0.0)
    eta_table = jnp.where(
        same_element & (node_column[:, None] == node_column[None, :]), along_eta, 0.0
    )
    return (xi_table, eta_table)


def plane_slopes(values, xi_table, eta_table, main_part, cross_part):
    flat_values = values.reshape(-1, 128)
    xi_slope = jnp.dot(flat_values, xi_table, precision=highest_precision).reshape(values.shape)
    eta_slope = jnp.dot(flat_values, eta_table, precision=highest_precision).reshape(values.shape)
    grad_x = main_part[0] * xi_slope + cross_part[0] * eta_slope
    grad_y = cross_part[1] * xi_slope + main_part[1] * eta_slope
    return (grad_x, grad_y)


def general_device(velocity, metric_main, metric_cross, stiffness, mass, precond, trace_map):
    rows_dev = velocity.shape[1]
    points = velocity.shape[2]
    patch_dev = trace_map.shape[0]
    width = stiffness.shape[1]
    trace_width = trace_map.shape[2]
    modes_dev = rows_dev // 2
    chebyshev = jnp.asarray(chebyshev_matrix(), jnp.float32)
    xi_table, eta_table = general_plane(chebyshev)
    basis_table, slope_table, forward, wave_all = general_spanwise()
    wave_rows = lax.dynamic_slice_in_dim(wave_all, lax.axis_index("mode") * rows_dev, rows_dev)
    damping = (1.0 + viscous_step * wave_rows * wave_rows)[None, :, None, None]
    patches = stiffness.reshape(patch_dev, width, width)
    inverse = precond.reshape(modes_dev, patch_dev, width, width)
    patch_mass = mass.reshape(patch_dev, width)
    point_numbers = jnp.arange(width, dtype=jnp.int32)[None, None, :]
    left_pick = (trace_map[:, 0][:, :, None] == point_numbers).astype(jnp.float32)
    right_pick = (trace_map[:, 1][:, :, None] == point_numbers).astype(jnp.float32)
    global_patch = lax.axis_index("elem") * patch_dev + jnp.arange(patch_dev)
    last_patch = patch_dev * lax.axis_size("elem") - 1
    left_gain = (global_patch > 0).astype(jnp.float32)[:, None]
    right_gain = (global_patch < last_patch).astype(jnp.float32)[:, None]
    multiplicity = (
        1.0 + left_gain * jnp.sum(left_pick, axis=1) + right_gain * jnp.sum(right_pick, axis=1)
    )
    weight = relaxation / (multiplicity * multiplicity)
    share = points // lax.axis_size("mode")
    main_share = lax.dynamic_slice_in_dim(metric_main, lax.axis_index("mode") * share, share, 1)
    cross_share = lax.dynamic_slice_in_dim(metric_cross, lax.axis_index("mode") * share, share, 1)

    def assemble(values):
        left_values = jnp.einsum("crpl,pjl->crpj", values, left_pick, precision=highest_precision)
        right_values = jnp.einsum("crpl,pjl->crpj", values, right_pick, precision=highest_precision)
        upward = shifted(right_values[:, :, -1].reshape(-1), "elem", 1)
        downward = shifted(left_values[:, :, 0].reshape(-1), "elem", -1)
        from_below = jnp.concatenate(
            [upward.reshape(3, rows_dev, 1, trace_width), right_values[:, :, :-1]], axis=2
        )
        from_above = jnp.concatenate(
            [left_values[:, :, 1:], downward.reshape(3, rows_dev, 1, trace_width)], axis=2
        )
        below_points = jnp.einsum(
            "crpj,pjl->crpl", from_below, left_pick, precision=highest_precision
        )
        above_points = jnp.einsum(
            "crpj,pjl->crpl", from_above, right_pick, precision=highest_precision
        )
        return values + below_points + above_points

    state = velocity
    for time_level in range(STEPS):
        coefficients = lax.all_to_all(state, "mode", split_axis=2, concat_axis=1, tiled=True)
        grad_x, grad_y = plane_slopes(coefficients, xi_table, eta_table, main_share, cross_share)
        plane_part = jnp.einsum(
            "frp,zr->fpz",
            jnp.concatenate([coefficients, grad_x, grad_y], axis=0),
            basis_table,
            precision=highest_precision,
        )
        spanwise_part = jnp.einsum(
            "frp,zr->fpz", coefficients, slope_table, precision=highest_precision
        )
        physical = jnp.concatenate([plane_part, spanwise_part], axis=0)
        advection = (
            physical[0:1] * physical[3:6]
            + physical[1:2] * physical[6:9]
            + physical[2:3] * physical[9:12]
        )
        advection_points = jnp.einsum(
            "ipz,rz->irp", advection, forward, precision=highest_precision
        )
        advection_hat = lax.all_to_all(
            advection_points, "mode", split_axis=1, concat_axis=2, tiled=True
        )
        source = (state - time_step * advection_hat).reshape(3, rows_dev, patch_dev, width)
        local_term = patch_mass * source
        iterate = jnp.zeros_like(source)
        for sweep_number in range(ITERS):
            if sweep_number == 0:
                residual = assemble(local_term)
            else:
                stiff_part = jnp.einsum(
                    "pij,crpj->crpi", patches, iterate, precision=highest_precision
                )
                residual = assemble(
                    local_term - viscous_step * stiff_part - damping * patch_mass * iterate
                )
            grouped = residual.reshape(3, modes_dev, 2, patch_dev, width)
            correction = jnp.einsum(
                "kpij,ckhpj->ckhpi", inverse, grouped, precision=highest_precision
            ).reshape(3, rows_dev, patch_dev, width)
            iterate = iterate + weight * assemble(correction)
        state = iterate.reshape(3, rows_dev, points)
    return state


def solution(mesh):
    return jax.shard_map(
        on_device,
        mesh=mesh,
        in_specs=(
            P(None, "mode", "elem"),
            P(None, "elem"),
            P(None, "elem"),
            P("elem", None),
            P("elem"),
            P("mode", "elem", None),
            P("elem", None, None),
        ),
        out_specs=P(None, "mode", "elem"),
        check_vma=False,
    )
```

profile of v0, /device:TPU:0, one launch (start us, length us, event | category | flops | bytes accessed | tf_op | source)
XLA Modules:
  0.0 135.3 jit_solution(911629234964589563)
XLA Ops:
  0.0 0.8 pad_bitcast_fusion.1
  0.8 0.6 copy.15
  1.4 132.2 %shard_map.136 = f32[3,16,1024]{2,1,0:T(8,128)} custom-call(f32[3,16,1024]{2,1,0:T(8,128)} %velocity.1, f32[2,1024]{1,0:T(2,128)} %metric_main.1, f32[2,1024]{1,0:T(2,128)} %metric_cross.1, f32[1024,512]{1,0:T(8,128)} %stiffness.1, f32[1,1024]{1,0:T(1,128)} %bitcast.7, s32[8,128]{1,0:T(8,128)} %bitcast.6, bf16[512,384]{1,0:T(8,128)(2,1)} %constant.16.clone.tables, ...), custom_call_target="tpu_custom_call" | custom-call | tf_op jit(solution)/shard_map/pallas_call | solution.py:548
  133.7 1.6 %copy.17 = f32[3,16,1024]{2,1,0:T(8,128)} copy(f32[3,16,1024]{2,1,0:T(8,128)} %shard_map.136) | data formatting | bytes 393216
  (1 shorter events, 0.0 us)
where the time goes:
time: 135 us
  Pallas kernels  132 us (98%)
  local copies, waits for them, and re-layouts  3.05 us (2%)
    pallas_call x1, Pallas kernels, on_device(): pl.pallas_call(functools.partial(kernel, ranks, depth, modes, patches, wi...  132 us

commit v1 on v0

--- a/solution.py
+++ b/solution.py
@@ -140,7 +140,7 @@
     metric_cross,
     stiffness,
     mass,
-    slots,
+    trace_map,
     tables,
     forward,
     plane,
@@ -158,6 +158,8 @@
     across,
     edge_high,
     edge_low,
+    beyond_high,
+    beyond_low,
     rows_high,
     rows_low,
     gate_high,
@@ -321,8 +323,11 @@
         multiplicity = jnp.ones((1, width), f32)
         for side in range(2):
             for kind in range(2):
-                line = (p * 2 + side) * 2 + kind
-                one_hot = jnp.where(slots[line : line + 1, :] == point, 1.0, 0.0)
+                ahead = jnp.full((1, trace * kind), -1, jnp.int32)
+                after = jnp.full((1, LANES - trace * (kind + 1)), -1, jnp.int32)
+                points = trace_map[p * 2 + side : p * 2 + side + 1, :]
+                slots = jnp.concatenate(([ahead] if kind else []) + [points, after], axis=1)
+                one_hot = jnp.where(slots == point, 1.0, 0.0)
                 turned = one_hot.T
                 pick[p, side, kind] = one_hot.astype(bf16)
                 pick_back[p, side, kind] = turned.astype(bf16)
@@ -336,6 +341,44 @@
     number = lax.broadcasted_iota(jnp.int32, (rows, 1), 0) // 8 + me * modes
     rate = 4.0 * number.astype(f32) / (modes * ranks)
     damped[...] = (1.0 + viscous_step * rate * rate) * mass[...]
+
+    def advect_send():
+        for offset in range(1, ranks):
+            coef_copy(offset).wait_recv()
+        own_coef().wait()
+        each = 2 * modes * ranks
+        fields = coef[...].reshape(3 * each, share)
+        high, low = split(fields)
+        slopes = dot(high, plane[0]) + dot(low, plane[0]) + dot(high, plane[1])
+        xi, eta = slopes[:, :share], slopes[:, share:]
+        mine = points_of(me)
+        grad_x = metric_main[0:1, mine] * xi + metric_cross[0:1, mine] * eta
+        grad_y = metric_cross[1:2, mine] * xi + metric_main[1:2, mine] * eta
+
+        def physical(table, values):
+            high, low = split(jnp.concatenate(values, axis=1))
+            return dot(table, jnp.concatenate([high, high, low], axis=0))
+
+        def part(value, c):
+            return value[c * each : (c + 1) * each]
+
+        plain = physical(tables[...], [part(fields, c) for c in range(3)])
+        u, v, w = (plain[:NZ, c * share : (c + 1) * share] for c in range(3))
+        for c in range(3):
+            slope = physical(tables[:NZ], [part(grad_x, c), part(grad_y, c)])
+            advection = (
+                u * slope[:, :share]
+                + v * slope[:, share:]
+                + w * plain[NZ:, c * share : (c + 1) * share]
+            )
+            high, low = split(advection)
+            total = dot(forward[0], high) + dot(forward[0], low) + dot(forward[1], high)
+            hat[pl.ds(2 * c, 2)] = total.reshape(2, modes * ranks, share)
+            for offset in range(1, ranks):
+                hat_copy(offset, c).start()
+        own_hat().start()
+
+    advect_send()
 
     def prepare(k, carry):
         span = pl.ds(pl.multiple_of(k * trace, trace), trace)
@@ -369,6 +412,9 @@
         gate_high[side, :, :wide] = rows_high[side].T.astype(bf16)
         gate_high[side, :, wide:] = pick[edge_patch[side], side, 0]
         gate_low[side] = rows_low[side].T.astype(bf16)
+        inward = across[0 if side == 0 else patches - 2, side]
+        beyond_high[side] = dot(edge_high[side], inward).astype(bf16)
+        beyond_low[side] = dot(edge_low[side], inward).astype(bf16)
     for side in range(2):
         @pl.when(has[side])
         def _():
@@ -401,41 +447,7 @@
             total = total + traced[:, start : start + LANES]
         return sent[:, wide:] + jnp.where(lane >= trace, repeated(total), 0.0)
 
-    def advect():
-        for offset in range(1, ranks):
-            coef_copy(offset).wait_recv()
-        own_coef().wait()
-        each = 2 * modes * ranks
-        fields = coef[...].reshape(3 * each, share)
-        high, low = split(fields)
-        slopes = dot(high, plane[0]) + dot(low, plane[0]) + dot(high, plane[1])
-        xi, eta = slopes[:, :share], slopes[:, share:]
-        mine = points_of(me)
-        grad_x = metric_main[0:1, mine] * xi + metric_cross[0:1, mine] * eta
-        grad_y = metric_cross[1:2, mine] * xi + metric_main[1:2, mine] * eta
-
-        def physical(table, values):
-            high, low = split(jnp.concatenate(values, axis=1))
-            return dot(table, jnp.concatenate([high, high, low], axis=0))
-
-        def part(value, c):
-            return value[c * each : (c + 1) * each]
-
-        plain = physical(tables[...], [part(fields, c) for c in range(3)])
-        u, v, w = (plain[:NZ, c * share : (c + 1) * share] for c in range(3))
-        for c in range(3):
-            slope = physical(tables[:NZ], [part(grad_x, c), part(grad_y, c)])
-            advection = (
-                u * slope[:, :share]
-                + v * slope[:, share:]
-                + w * plain[NZ:, c * share : (c + 1) * share]
-            )
-            high, low = split(advection)
-            total = dot(forward[0], high) + dot(forward[0], low) + dot(forward[1], high)
-            hat[pl.ds(2 * c, 2)] = total.reshape(2, modes * ranks, share)
-            for offset in range(1, ranks):
-                hat_copy(offset, c).start()
-        own_hat().start()
+    def advect_receive():
         for offset in range(1, ranks):
             coef_copy(offset).wait_send()
             for c in range(3):
@@ -468,39 +480,52 @@
                 )
             terms.append(term)
         lines = [both(term) for term in assembled(terms)]
-        notes = []
+
+        def corrected(p, k):
+            line = lines[p][k * 16 : (k + 1) * 16]
+            return dot(line, inverse_high[k, p]) + dot(line, inverse_low[k, p])
+
+        blocks = [(p, k) for p in range(patches) for k in range(modes)]
+        early, late = len(blocks) // 4, len(blocks) - len(blocks) // 4
+        found = {}
+        notes = [noted(lines[edge_patch[side]], side) for side in range(2)]
         for side in range(2):
-            note = noted(lines[edge_patch[side]], side)
-            note_out[side] = note
-            notes.append(note)
+            note_out[side] = notes[side]
+        for block in blocks[:early]:
+            found[block] = corrected(*block)
         for side in range(2):
             @pl.when(has[side])
             def _():
                 note_copy(side, slot).start()
-        parts = []
-        for p in range(patches):
-            found = []
-            for k in range(modes):
-                line = lines[p][k * 16 : (k + 1) * 16]
-                found.append(dot(line, inverse_high[k, p]) + dot(line, inverse_low[k, p]))
-            parts.append(folded(jnp.concatenate(found, axis=0)))
+        for block in blocks[early:late]:
+            found[block] = corrected(*block)
         near = [product(spread(notes[side]), corner_high[side], corner_low[side]) for side in range(2)]
         for side in range(2):
             @pl.when(has[side])
             def _():
                 note_wait(side, slot)
-        gains = []
+        gains = [jnp.zeros((rows, width), f32)] * patches
         for side in range(2):
-            p = edge_patch[side]
+            p, inner = edge_patch[side], edge_patch[side] + 1 - 2 * side
             note = note_in[slot, side]
-            parts[p] = parts[p] + product(spread(note), edge_high[side], edge_low[side])
-            gains.append(moved(note + near[side], pick_back[p, side, 1]))
+            spread_note = both(spread(note))
+            gains[p] = gains[p] + folded(
+                dot(spread_note, edge_high[side])
+                + dot(spread_note, edge_low[side])
+                + dot(both(note + near[side]), pick_back[p, side, 1])
+            )
+            gains[inner] = gains[inner] + folded(
+                dot(spread_note, beyond_high[side]) + dot(spread_note, beyond_low[side])
+            )
+        for block in blocks[late:]:
+            found[block] = corrected(*block)
+        parts = [
+            folded(jnp.concatenate([found[p, k] for k in range(modes)], axis=0))
+            for p in range(patches)
+        ]
         total = assembled(parts)
-        for side in range(2):
-            p = edge_patch[side]
-            total[p] = total[p] + gains[side]
         for p in range(patches):
-            step = weight[:, patch_of(p)] * total[p]
+            step = weight[:, patch_of(p)] * (total[p] + gains[p])
             iterate[:, patch_of(p)] = step if first else iterate[:, patch_of(p)] + step
 
     def later_sweep(number, carry):
@@ -508,7 +533,7 @@
         return carry
 
     def level(number, carry):
-        advect()
+        advect_receive()
         sweep(0, True)
         lax.fori_loop(1, ITERS, later_sweep, 0)
         state[...] = reordered(back[...], iterate[...]).reshape(6, modes, patches * width)
@@ -516,6 +541,7 @@
         @pl.when(number < STEPS - 1)
         def _():
             send_coef()
+            advect_send()
 
         return carry
 
@@ -534,13 +560,6 @@
         return general_device(
             velocity, metric_main, metric_cross, stiffness, mass, precond, trace_map
         )
-    slots = jnp.stack(
-        [
-            jnp.pad(trace_map, ((0, 0), (0, 0), (0, LANES - trace)), constant_values=-1),
-            jnp.pad(trace_map, ((0, 0), (0, 0), (trace, LANES - 2 * trace)), constant_values=-1),
-        ],
-        axis=2,
-    )
     basis, slope, forward = spanwise_tables(modes * ranks)
     vmem = pl.BlockSpec(memory_space=pltpu.VMEM)
     wide = modes * trace
@@ -557,6 +576,8 @@
             pltpu.VMEM((patches, width, width), bf16),
             pltpu.VMEM((patches, width, width), bf16),
             pltpu.VMEM((patches - 1, 2, width, width), bf16),
+            pltpu.VMEM((2, wide, width), bf16),
+            pltpu.VMEM((2, wide, width), bf16),
             pltpu.VMEM((2, wide, width), bf16),
             pltpu.VMEM((2, wide, width), bf16),
             pltpu.VMEM((2, wide, width), f32),
@@ -599,7 +620,7 @@
         metric_cross,
         stiffness,
         mass.reshape(1, points),
-        slots.reshape(patches * 4, LANES),
+        trace_map.reshape(patches * 2, trace),
         jnp.asarray(np.concatenate([basis, slope], axis=0)),
         jnp.asarray(forward),
         jnp.asarray(plane_tables()),

time: 135 us -> 148 us (1.096)
  Pallas kernels: 132 us -> 147 us
    pallas_call x1, Pallas kernels: 132 us -> 147 us  [on_device(): pl.pallas_call(functools.partial(kernel, ranks, depth, modes, patches, wi...]
where the time goes in v1:
time: 148 us
  Pallas kernels  147 us (99%)
  local copies, waits for them, and re-layouts  1.62 us (1%)
    pallas_call x1, Pallas kernels, on_device(): pl.pallas_call(functools.partial(kernel, ranks, depth, modes, patches, wi...  147 us

profile of v1, /device:TPU:0, one launch (start us, length us, event | category | flops | bytes accessed | tf_op | source)
XLA Modules:
  0.0 148.2 jit_solution(8695774573563792143)
XLA Ops:
  0.0 146.6 %shard_map.136 = f32[3,16,1024]{2,1,0:T(8,128)} custom-call(f32[3,16,1024]{2,1,0:T(8,128)} %velocity.1, f32[2,1024]{1,0:T(2,128)} %metric_main.1, f32[2,1024]{1,0:T(2,128)} %metric_cross.1, f32[1024,512]{1,0:T(8,128)} %stiffness.1, f32[1,1024]{1,0:T(1,128)} %bitcast.2, s32[4,32]{1,0:T(4,128)} %bitcast.3, bf16[512,384]{1,0:T(8,128)(2,1)} %constant.14.clone.tables, ...), custom_call_target="tpu_custom_call" | custom-call | tf_op jit(solution)/shard_map/pallas_call | solution.py:567
  146.6 1.6 %copy.16 = f32[3,16,1024]{2,1,0:T(8,128)} copy(f32[3,16,1024]{2,1,0:T(8,128)} %shard_map.136) | data formatting | bytes 393216

commit v2 on v1

--- a/solution.py
+++ b/solution.py
@@ -427,6 +427,15 @@
         == lax.broadcasted_iota(jnp.int32, (rows, wide), 1) // trace
     )
 
+    def packed(note):
+        half = rows // 2
+        return jnp.where(
+            lane[:half] < LANES // 2, note[:half], pltpu.roll(note[half:], LANES // 2, 1)
+        )
+
+    def unpacked(note):
+        return jnp.concatenate([note, pltpu.roll(note, LANES // 2, 1)], axis=0)
+
     def repeated(value):
         total = value
         for turn in range(1, LANES // trace):
@@ -485,20 +494,18 @@
             line = lines[p][k * 16 : (k + 1) * 16]
             return dot(line, inverse_high[k, p]) + dot(line, inverse_low[k, p])
 
-        blocks = [(p, k) for p in range(patches) for k in range(modes)]
-        early, late = len(blocks) // 4, len(blocks) - len(blocks) // 4
-        found = {}
         notes = [noted(lines[edge_patch[side]], side) for side in range(2)]
         for side in range(2):
-            note_out[side] = notes[side]
-        for block in blocks[:early]:
-            found[block] = corrected(*block)
+            note_out[side] = packed(notes[side])
         for side in range(2):
             @pl.when(has[side])
             def _():
                 note_copy(side, slot).start()
-        for block in blocks[early:late]:
-            found[block] = corrected(*block)
+        parts = []
+        for p in range(patches):
+            found = [corrected(p, k) for k in range(modes)]
+            parts.append(folded(jnp.concatenate(found, axis=0)))
+        total = assembled(parts)
         near = [product(spread(notes[side]), corner_high[side], corner_low[side]) for side in range(2)]
         for side in range(2):
             @pl.when(has[side])
@@ -507,7 +514,7 @@
         gains = [jnp.zeros((rows, width), f32)] * patches
         for side in range(2):
             p, inner = edge_patch[side], edge_patch[side] + 1 - 2 * side
-            note = note_in[slot, side]
+            note = unpacked(note_in[slot, side])
             spread_note = both(spread(note))
             gains[p] = gains[p] + folded(
                 dot(spread_note, edge_high[side])
@@ -517,13 +524,6 @@
             gains[inner] = gains[inner] + folded(
                 dot(spread_note, beyond_high[side]) + dot(spread_note, beyond_low[side])
             )
-        for block in blocks[late:]:
-            found[block] = corrected(*block)
-        parts = [
-            folded(jnp.concatenate([found[p, k] for k in range(modes)], axis=0))
-            for p in range(patches)
-        ]
-        total = assembled(parts)
         for p in range(patches):
             step = weight[:, patch_of(p)] * (total[p] + gains[p])
             iterate[:, patch_of(p)] = step if first else iterate[:, patch_of(p)] + step
@@ -556,7 +556,7 @@
     patches, _, trace = trace_map.shape
     width = stiffness.shape[1]
     share = points // ranks
-    if modes % 8 or share != LANES or LANES % trace or (modes * trace) % LANES or patches < 2:
+    if modes % 8 or share != LANES or LANES != 4 * trace or (modes * trace) % LANES or patches < 2:
         return general_device(
             velocity, metric_main, metric_cross, stiffness, mass, precond, trace_map
         )
@@ -598,8 +598,8 @@
             pltpu.VMEM((8 * modes, points), f32),
             pltpu.VMEM((1, points), f32),
             pltpu.VMEM((8 * modes, points), f32),
-            pltpu.VMEM((2, 8 * modes, LANES), f32),
-            pltpu.VMEM((2, 2, 8 * modes, LANES), f32),
+            pltpu.VMEM((2, 4 * modes, LANES), f32),
+            pltpu.VMEM((2, 2, 4 * modes, LANES), f32),
             pltpu.SemaphoreType.DMA((modes, patches)),
             pltpu.SemaphoreType.DMA((2,)),
             pltpu.SemaphoreType.DMA((ranks,)),

time: 148 us -> 133 us (0.90)
  Pallas kernels: 147 us -> 131 us
    pallas_call x1, Pallas kernels: 147 us -> 131 us  [on_device(): pl.pallas_call(functools.partial(kernel, ranks, depth, modes, patches, wi...]
where the time goes in v2:
time: 133 us
  Pallas kernels  131 us (98%)
  local copies, waits for them, and re-layouts  1.62 us (1%)
    pallas_call x1, Pallas kernels, on_device(): pl.pallas_call(functools.partial(kernel, ranks, depth, modes, patches, wi...  131 us

profile of v2, /device:TPU:0, one launch (start us, length us, event | category | flops | bytes accessed | tf_op | source)
XLA Modules:
  0.0 133.0 jit_solution(4229781858515307363)
XLA Ops:
  0.0 131.3 %shard_map.136 = f32[3,16,1024]{2,1,0:T(8,128)} custom-call(f32[3,16,1024]{2,1,0:T(8,128)} %velocity.1, f32[2,1024]{1,0:T(2,128)} %metric_main.1, f32[2,1024]{1,0:T(2,128)} %metric_cross.1, f32[1024,512]{1,0:T(8,128)} %stiffness.1, f32[1,1024]{1,0:T(1,128)} %bitcast.2, s32[4,32]{1,0:T(4,128)} %bitcast.3, bf16[512,384]{1,0:T(8,128)(2,1)} %constant.14.clone.tables, ...), custom_call_target="tpu_custom_call" | custom-call | tf_op jit(solution)/shard_map/pallas_call | solution.py:567
  131.4 1.6 %copy.16 = f32[3,16,1024]{2,1,0:T(8,128)} copy(f32[3,16,1024]{2,1,0:T(8,128)} %shard_map.136) | data formatting | bytes 393216

commit v3 on v2

--- a/solution.py
+++ b/solution.py
@@ -497,13 +497,15 @@
         notes = [noted(lines[edge_patch[side]], side) for side in range(2)]
         for side in range(2):
             note_out[side] = packed(notes[side])
+        first_found = [corrected(0, k) for k in range(2)]
         for side in range(2):
             @pl.when(has[side])
             def _():
                 note_copy(side, slot).start()
         parts = []
         for p in range(patches):
-            found = [corrected(p, k) for k in range(modes)]
+            found = list(first_found) if p == 0 else []
+            found += [corrected(p, k) for k in range(len(found), modes)]
             parts.append(folded(jnp.concatenate(found, axis=0)))
         total = assembled(parts)
         near = [product(spread(notes[side]), corner_high[side], corner_low[side]) for side in range(2)]

time: 133 us -> 133 us (level)
  no operation moved by 1% of the time
where the time goes in v3:
time: 133 us
  Pallas kernels  131 us (98%)
  local copies, waits for them, and re-layouts  1.62 us (1%)
    pallas_call x1, Pallas kernels, on_device(): pl.pallas_call(functools.partial(kernel, ranks, depth, modes, patches, wi...  131 us

profile of v3, /device:TPU:0, one launch (start us, length us, event | category | flops | bytes accessed | tf_op | source)
XLA Modules:
  0.0 133.1 jit_solution(10140729835529279910)
XLA Ops:
  0.0 131.4 %shard_map.136 = f32[3,16,1024]{2,1,0:T(8,128)} custom-call(f32[3,16,1024]{2,1,0:T(8,128)} %velocity.1, f32[2,1024]{1,0:T(2,128)} %metric_main.1, f32[2,1024]{1,0:T(2,128)} %metric_cross.1, f32[1024,512]{1,0:T(8,128)} %stiffness.1, f32[1,1024]{1,0:T(1,128)} %bitcast.2, s32[4,32]{1,0:T(4,128)} %bitcast.3, bf16[512,384]{1,0:T(8,128)(2,1)} %constant.14.clone.tables, ...), custom_call_target="tpu_custom_call" | custom-call | tf_op jit(solution)/shard_map/pallas_call | solution.py:569
  131.4 1.6 %copy.16 = f32[3,16,1024]{2,1,0:T(8,128)} copy(f32[3,16,1024]{2,1,0:T(8,128)} %shard_map.136) | data formatting | bytes 393216
